TPU v7x, 32 devices: a whole 2x2x4 slice. The times are simulated.
32 devices in a mesh: frag: 1, alpha: 8 (over z, y), beta: 2 (over x), orb: 2 (over core).
Axes of the slice: x: 2, y: 2, z: 4, core: 2. Of those that a mesh axis runs over, the one named last changes fastest.
Arguments:
- civec: bfloat16 [2048, 8192], P(('frag', 'alpha'), ('beta', 'orb')), may hold values from -1 to 1
- alpha_coupling: bfloat16 [96, 128, 128], P('frag'), may hold values from -0.5 to 0.5
- alpha_source: int32 [96], P('frag'), may hold values from 0 to 15
- alpha_pair: int32 [96], P('frag'), may hold values from 0 to 783
- alpha_count: int32 [16], P('frag'), may hold values from 1 to 6, 64 in all
- beta_coupling: bfloat16 [1024, 128, 128], P(('frag', 'beta', 'orb')), may hold values from -0.5 to 0.5
- beta_source: int32 [1024], P(('frag', 'beta', 'orb')), may hold values from 0 to 63
- beta_pair: int32 [1024], P(('frag', 'beta', 'orb')), may hold values from 0 to 783
- beta_count: int32 [64], P(('frag', 'beta', 'orb')), may hold values from 1 to 16, 682 in all
Outputs:
- gamma: float32 [2, 784, 784], P('frag', 'alpha', ('beta', 'orb'))
All inputs are finite; a program needn't handle non-finite values. No bound on the sum of `beta_count` on one device may be relied on, other than what follows from the above.
Results may differ from a plain program's by a relative error of at most 0.0003.
Values may be sent and summed in bfloat16 or wider, within the bound.
A program may use at most 192 MiB of HBM per device.

v0:
```python
import jax
import jax.numpy as jnp
from jax import lax
from jax.sharding import PartitionSpec as P

NPAIR = 784


def occupied_slots(filled, slots):
    marks = jnp.arange(slots, dtype=jnp.int32)[None, :] < filled[:, None]
    return marks.reshape(-1).astype(jnp.float32)


def pair_density(grams, pair_index):
    units, slots, _ = grams.shape
    onehot = (pair_index[:, None] == jnp.arange(NPAIR, dtype=jnp.int32)[None, :]).astype(
        jnp.float32
    )
    onehot = onehot.reshape(units, slots, NPAIR)
    weighted = jnp.einsum("ukl,ulq->ukq", grams, onehot, precision=lax.Precision.HIGHEST)
    return jnp.einsum("ukp,ukq->pq", onehot, weighted, precision=lax.Precision.HIGHEST)


def alpha_grams(blocks, couplings, sources, filled):
    slots = sources.shape[0] // filled.shape[0]
    picked = jnp.take(blocks, sources, axis=0)
    images = jnp.einsum("sij,sjw->siw", couplings, picked, preferred_element_type=jnp.float32)
    occupied = occupied_slots(filled, slots)
    images = (images * occupied[:, None, None]).astype(jnp.bfloat16)
    grouped = images.reshape(filled.shape[0], slots, -1)
    return jnp.einsum("ukm,ulm->ukl", grouped, grouped, preferred_element_type=jnp.float32)


def body(
    civec,
    alpha_coupling,
    alpha_source,
    alpha_pair,
    alpha_count,
    beta_coupling,
    beta_source,
    beta_pair,
    beta_count,
):
    local_rows, local_cols = civec.shape
    block_size = alpha_coupling.shape[1]
    alpha_slots = alpha_source.shape[0] // alpha_count.shape[0]
    gathered = lax.all_gather(civec, "alpha", axis=0, tiled=True)
    blocks = gathered.reshape(-1, block_size, local_cols)
    targets = local_rows // block_size
    opening = lax.axis_index("alpha") * targets
    couplings = lax.dynamic_slice_in_dim(
        alpha_coupling, opening * alpha_slots, targets * alpha_slots, 0
    )
    sources = lax.dynamic_slice_in_dim(
        alpha_source, opening * alpha_slots, targets * alpha_slots, 0
    )
    pair_index = lax.dynamic_slice_in_dim(
        alpha_pair, opening * alpha_slots, targets * alpha_slots, 0
    )
    filled = lax.dynamic_slice_in_dim(alpha_count, opening, targets, 0)
    alpha_gram = alpha_grams(blocks, couplings, sources, filled)
    panel = lax.all_gather(civec, ("beta", "orb"), axis=1, tiled=True).reshape(
        local_rows, -1, block_size
    )
    beta_slots = beta_source.shape[0] // beta_count.shape[0]
    picked = jnp.take(panel, beta_source, axis=1)
    images = jnp.einsum("rsj,skj->srk", picked, beta_coupling, preferred_element_type=jnp.float32)
    occupied = occupied_slots(beta_count, beta_slots)
    images = (images * occupied[:, None, None]).astype(jnp.bfloat16)
    grouped = images.reshape(beta_count.shape[0], beta_slots, -1)
    beta_gram = jnp.einsum("ukm,ulm->ukl", grouped, grouped, preferred_element_type=jnp.float32)
    gamma_alpha = pair_density(alpha_gram, pair_index)
    gamma_beta = pair_density(beta_gram, beta_pair)
    partial_sums = jnp.stack([gamma_alpha, gamma_beta])
    reduced = lax.psum_scatter(partial_sums, "alpha", scatter_dimension=1, tiled=True)
    return lax.psum_scatter(reduced, ("beta", "orb"), scatter_dimension=2, tiled=True)


def solution(mesh):
    return jax.shard_map(
        body,
        mesh=mesh,
        in_specs=(
            P(("frag", "alpha"), ("beta", "orb")),
            P("frag", None, None),
            P("frag"),
            P("frag"),
            P("frag"),
            P(("frag", "beta", "orb"), None, None),
            P(("frag", "beta", "orb")),
            P(("frag", "beta", "orb")),
            P(("frag", "beta", "orb")),
        ),
        out_specs=P("frag", "alpha", ("beta", "orb")),
        check_vma=False,
    )
```

profile of v0, /device:TPU:0, one launch (start us, length us, event | category | flops | bytes accessed | tf_op | source)
XLA Modules:
  0.0 462.7 jit_solution(6049405173240906632)
XLA Ops:
  6.5 2.4 copy.20
  9.0 0.0 all-gather.5.cloned.1.call-update
  9.0 0.0 all-gather.3.cloned.1.call-start
  9.0 0.7 all-gather.3.cloned.1.call-update
  9.7 0.0 all-reduce.5.cloned.1.call-start
  9.8 0.7 fusion.20
  10.5 0.1 reshape.81
  10.6 0.8 eq.36
  11.3 0.1 copy.19
  11.4 0.7 dynamic_slice.15
  12.2 0.1 compare_convert_fusion
  12.2 0.1 reshape.80
  12.3 0.7 dynamic_slice.12
  13.0 0.1 eq.32
  13.1 0.7 compare_and_fusion.1
  13.9 0.7 compare_select_fusion
  14.6 0.7 compare_and_fusion
  15.2 0.2 iota_compare_fusion
  15.4 30.9 %all-gather.5.cloned.1.call-done = bf16[256,8192]{0,1:T(8,128)(2,1)} async-done(((bf16[256,2048]{0,1:T(8,128)(2,1)}), bf16[256,8192]{0,1:T(8,128)(2,1)}) %all-gather.5.cloned.1.call-update) | async-done | bytes 4194320 | tf_op jit(solution)/shard_map/all_gather | solution.py:63
  46.3 6.3 %copy.21 = bf16[256,64,128]{2,0,1:T(8,128)(2,1)} copy(bf16[256,64,128]{0,2,1:T(8,128)(2,1)} %bitcast.24) | data formatting | bytes 8388608 | tf_op jit(solution)/shard_map/reshape | solution.py:63
  52.7 12.0 %gather_fusion.1 = bf16[256,256,128]{2,1,0:T(8,128)(2,1)} fusion(bf16[256,64,128]{2,0,1:T(8,128)(2,1)} %copy.21, s32[1024]{0:T(1024)S(1)} %pad_clamp_fusion), kind=kCustom, calls=%fused_computation.1 | custom fusion | bytes 33555456 | tf_op jit(solution)/shard_map/jit(_take)/gather | solution.py:67
  64.6 16.9 %multiply_convert_fusion = bf16[256,256,128]{2,1,0:T(8,128)(2,1)} fusion(f32[256]{0:T(256)S(1)} %reshape.81, bf16[256,128,128]{2,1,0:T(8,128)(2,1)} %param.14, bf16[256,256,128]{2,1,0:T(8,128)(2,1)} %gather_fusion.1, pred[256]{0:T(512)(128)(4,1)S(1)} %compare_and_fusion), kind=kOutput, calls=%fused_computation.2 | convolution fusion | flops 2172649472 | bytes 41944320 | tf_op jit(solution)/shard_map/rsj,skj->srk/dot_general | solution.py:68
  81.5 25.5 %reshape.79 = bf16[16,16,32768]{2,1,0:T(8,128)(2,1)} reshape(bf16[256,256,128]{2,1,0:T(8,128)(2,1)} %multiply_convert_fusion) | data formatting | bytes 33554432 | tf_op jit(solution)/shard_map/reshape | solution.py:71
  107.0 17.5 %fusion.25 = f32[16,16,16]{2,1,0:T(8,128)S(1)} fusion(bf16[16,16,32768]{2,1,0:T(8,128)(2,1)} %reshape.79), kind=kOutput, calls=%fused_computation.40 | convolution fusion | flops 268435456 | bytes 16793600 | tf_op jit(solution)/shard_map/ukm,ulm->ukl/dot_general | solution.py:72
  124.5 0.5 fusion.14
  125.0 3.3 convolution_bitcast_fusion
  128.3 45.1 %all-gather.3.cloned.1.call-done = bf16[2048,2048]{1,0:T(8,128)(2,1)} async-done(((bf16[256,2048]{1,0:T(8,128)(2,1)}), bf16[2048,2048]{1,0:T(8,128)(2,1)}) %all-gather.3.cloned.1.call-update) | async-done | bytes 8388624 | tf_op jit(solution)/shard_map/all_gather | solution.py:48
  173.4 7.5 %gather_fusion = bf16[12,128,2048]{2,1,0:T(8,128)(2,1)} fusion(bf16[16,128,2048]{2,1,0:T(8,128)(2,1)} %bitcast.23, s32[1024]{0:T(1024)S(1)} %pad_clamp_fusion.1), kind=kCustom, calls=%fused_computation | custom fusion | bytes 12582960 | tf_op jit(solution)/shard_map/jit(_take)/gather | solution.py:26
  181.0 7.3 %multiply_convert_fusion.1 = bf16[12,128,2048]{2,1,0:T(8,128)(2,1)} fusion(f32[12]{0:T(128)S(1)} %reshape.80, bf16[12,128,2048]{2,1,0:T(8,128)(2,1)} %gather_fusion, pred[12]{0:T(512)(128)(4,1)S(1)} %get-tuple-element.5, bf16[96,128,128]{2,1,0:T(8,128)(2,1)S(1)} %copy-done, s32[]{:T(128)S(6)} %select_n.26), kind=kOutput, calls=%fused_computation.7 | convolution fusion | flops 814743552 | bytes 12977156 | tf_op jit(solution)/shard_map/sij,sjw->siw/dot_general | solution.py:27
  188.3 13.6 %reshape.77 = bf16[2,6,262144]{2,1,0:T(8,128)(2,1)} reshape(bf16[12,128,2048]{2,1,0:T(8,128)(2,1)} %multiply_convert_fusion.1) | data formatting | bytes 12582912 | tf_op jit(solution)/shard_map/reshape | solution.py:30
  201.9 11.3 %fusion.24 = f32[2,6,6]{2,1,0:T(8,128)S(1)} fusion(bf16[2,6,262144]{2,1,0:T(8,128)(2,1)} %reshape.77), kind=kOutput, calls=%fused_computation.39 | convolution fusion | flops 37748736 | bytes 6291744 | tf_op jit(solution)/shard_map/ukm,ulm->ukl/dot_general | solution.py:31
  213.2 0.2 fusion.17
  213.4 1.6 convolution_bitcast_fusion.1
  215.0 2.2 pad_maximum_fusion
  217.2 0.0 copy-start.2
  217.2 0.0 copy-start.1
  217.2 5.4 %copy.24 = f32[2,784,784]{2,0,1:T(2,128)} copy(f32[2,784,784]{2,1,0:T(8,128)S(1)} %pad_maximum_fusion) | data formatting | bytes 9834496 | tf_op jit(solution)/shard_map/stack | solution.py:75
  222.6 0.0 all-reduce.5.cloned.1.call-update
  222.7 0.0 all-reduce.7.cloned.1.call-start
  222.7 0.6 dynamic-slice
  224.0 191.6 %all-reduce.5.cloned.1.call-done = f32[2,784,784]{2,0,1:T(2,128)} async-done(((f32[2,784,784]{2,0,1:T(2,128)}), f32[2,784,784]{2,0,1:T(2,128)}) %all-reduce.5.cloned.1.call-update) | async-done | bytes 4917264
  415.6 2.1 constant_dynamic-slice_fusion.1
  417.6 2.9 copy.25
  420.5 0.0 all-reduce.7.cloned.1.call-update
  420.6 0.6 dynamic-slice.2
  421.8 32.6 %all-reduce.7.cloned.1.call-done = f32[2,98,784]{1,0,2:T(2,128)} async-done(((f32[2,98,784]{1,0,2:T(2,128)}), f32[2,98,784]{1,0,2:T(2,128)}) %all-reduce.7.cloned.1.call-update) | async-done | bytes 614672
  454.4 0.9 constant_dynamic-slice_fusion
  455.3 0.8 copy.26
  (7 shorter events, 0.0 us)
Async XLA Ops:
  6.5 174.4 %copy-start = (bf16[96,128,128]{2,1,0:T(8,128)(2,1)S(1)}, bf16[96,128,128]{2,1,0:T(8,128)(2,1)}, u32[]{:S(2)}) copy-start(bf16[96,128,128]{2,1,0:T(8,128)(2,1)} %param.10) | copy-start | bytes 9437188
  6.5 39.8 %all-gather.5.cloned.1.call-start = ((), (), s32[]{:S(2)}) async-start(), calls=%async_computation.1 | async-start | bytes 5242880 | tf_op jit(solution)/shard_map/all_gather | solution.py:63
  9.0 164.4 %all-gather.3.cloned.1.call-start = ((), (), s32[]{:S(2)}) async-start(), calls=%async_computation | async-start | bytes 9437184 | tf_op jit(solution)/shard_map/all_gather | solution.py:48
  9.7 405.8 %all-reduce.5.cloned.1.call-start = ((), (), s32[]{:S(2)}) async-start(), calls=%async_computation.2 | async-start | bytes 11239424
  217.2 5.5 %copy-start.2 = (u32[32]{0:T(128)S(1)}, u32[32]{0:T(128)}, u32[]{:S(2)}) copy-start(u32[32]{0:T(128)} %constant.47) | copy-start | bytes 388
  217.2 203.3 %copy-start.1 = (u32[32]{0:T(128)S(1)}, u32[32]{0:T(128)}, u32[]{:S(2)}) copy-start(u32[32]{0:T(128)} %constant.51) | copy-start | bytes 388
  222.7 231.7 %all-reduce.7.cloned.1.call-start = ((), (), s32[]{:S(2)}) async-start(), calls=%async_computation.3 | async-start | bytes 1605632
Sparse Core Ops, SparseCore 0:
  9.1 37.1 all-gather.4
  48.4 124.9 all-gather.2
  222.8 192.7 all-reduce.4
  420.7 33.6 all-reduce.6
where the time goes:
time: 464 us; the launch traced here: 463 us
  waiting for transfers between devices  301 us (65%)
  local copies, waits for them, and re-layouts  83.3 us (18%)
  matrix products  58.6 us (13%)
  between operations  14.5 us (3%)
  other arithmetic  5.27 us (1%)
    unnamed x6, waiting for transfers between devices  225 us
    all_gather x1, waiting for transfers between devices, body(): gathered = lax.all_gather(civec, 'alpha', axis=0, tiled=True)  45.1 us
    all_gather x1, waiting for transfers between devices, body(): lax.all_gather(civec, ('beta', 'orb'), axis=1, tiled=True)  30.9 us
    reshape x1, local copies, waits for them, and re-layouts, body(): grouped = images.reshape(beta_count.shape[0], beta_slots, -1)  25.5 us
    dot_general x1, matrix products, body(): jnp.einsum('ukm,ulm->ukl', grouped, grouped, preferred_element_type=jnp.f...  17.5 us
    dot_general x1, matrix products, body(): jnp.einsum('rsj,skj->srk', picked, beta_coupling, preferred_element_type=...  16.9 us
    reshape x1, local copies, waits for them, and re-layouts, alpha_grams(): grouped = images.reshape(filled.shape[0], slots, -1)  13.6 us
    gather x1, local copies, waits for them, and re-layouts, body(): picked = jnp.take(panel, beta_source, axis=1)  12 us
  transfers between devices with their start and end apart: 4, of which 4 were waited for; matrix products, arithmetic and copies ran while one was open for 19% of the time, Pallas kernels for 0%

commit v1 on v0

v1 whole, which is shorter than its diff:
```python
import functools

import jax
import jax.numpy as jnp
from jax import lax
from jax.experimental import pallas as pl
from jax.experimental.pallas import tpu as pltpu
from jax.sharding import PartitionSpec as P

NPAIR = 784
MESH = pl.DeviceIdType.MESH
F32 = jnp.float32
BF16 = jnp.bfloat16
LANES = 128
ROWT = 16


def up(n, m):
    return -(-n // m) * m


def dot_nt(x, y):
    return lax.dot_general(x, y, (((1,), (1,)), ((), ())), preferred_element_type=F32)


def dot_nn(x, y):
    return jnp.dot(x, y, preferred_element_type=F32)


def halves(x):
    hi = x.astype(BF16)
    return hi, (x - hi.astype(F32)).astype(BF16)


def iota(shape, dim):
    return lax.broadcasted_iota(jnp.int32, shape, dim)


def kernel(
    cfg, civec, acoup_hbm, asrc, apair, acnt, bcoup_hbm, bsrc, bpair, bcnt, out, *scratch
):
    na, nb, no, chunks, capa, capb, ta, tb, width, cols = cfg
    nbo = nb * no
    nq = len(chunks)
    panels = scratch[:nq]
    (
        acol, acoup, bcoup, ybuf, yabuf, vb, va, pall, gloc, rsbuf, exbuf, gsum,
        lsem, psem, xs, xr, os_, or_, fs, fr, als, alr, ps, pr, rss, rsr, exs, exr, ags, agr,
    ) = scratch[nq:]
    a = lax.axis_index("alpha")
    b = lax.axis_index("beta")
    o = lax.axis_index("orb")
    bo = b * no + o
    other = 1 - o
    row0 = [sum(chunks[:q]) for q in range(nq)]

    wide = cols // LANES

    def section(q, which):
        return panels[q].at[pl.ds(which * wide, wide)]

    def remote(src, dst, ss, rs, dev):
        return pltpu.make_async_remote_copy(
            src_ref=src, dst_ref=dst, send_sem=ss, recv_sem=rs,
            device_id=dev, device_id_type=MESH,
        )

    local = [
        [
            pltpu.make_async_copy(
                civec.at[row0[q] // LANES, pl.ds(row0[q] % LANES, chunks[q]), pl.ds(i * LANES, LANES)],
                panels[q].at[bo * wide + i], psem.at[q, i])
            for i in range(wide)
        ]
        for q in range(nq)
    ]
    bcopy = pltpu.make_async_copy(bcoup_hbm, bcoup, lsem.at[0])
    acopy = pltpu.make_async_copy(acoup_hbm, acoup, lsem.at[1])
    tall = civec.shape[0]
    ownrows = acol.at[pl.ds(a * tall, tall)]
    owncols = pltpu.make_async_copy(
        civec.at[:, :, pl.ds(pl.multiple_of(a * width, LANES), width)], ownrows, lsem.at[2])
    ownpair = pltpu.make_async_copy(bpair, pall.at[bo], lsem.at[3])

    barrier = pltpu.get_barrier_semaphore()
    for d in range(1, na):
        pl.semaphore_signal(barrier, inc=1, device_id={"alpha": lax.rem(a + d, na)}, device_id_type=MESH)
    for d in range(1, nbo):
        peer = lax.rem(bo + d, nbo)
        pl.semaphore_signal(
            barrier, inc=1,
            device_id={"beta": lax.div(peer, no), "orb": lax.rem(peer, no)}, device_id_type=MESH)
    for q in range(nq):
        for c in local[q]:
            c.start()
    ownpair.start()
    owncols.start()
    bcopy.start()
    acopy.start()
    pl.semaphore_wait(barrier, na - 1 + nbo - 1)

    xcopies, ocopies, fcopies, acopies, pcopies = {}, {}, {}, [], []
    for q in range(nq):
        for c in local[q]:
            c.wait()
        mine = section(q, bo)
        for d in range(1, nb):
            c = remote(mine, mine, xs.at[q, d], xr.at[q, d],
                       {"beta": lax.rem(b + d, nb)})
            c.start()
            xcopies[q, d] = c
        if q == 0:
            for d in range(1, na):
                peer = lax.rem(a + d, na)
                c = remote(
                    civec.at[:, :, pl.ds(pl.multiple_of(peer * width, LANES), width)], ownrows,
                    als.at[d], alr.at[d], {"alpha": peer})
                c.start()
                acopies.append(c)
        c = remote(mine, mine, os_.at[q], or_.at[q], {"orb": other})
        c.start()
        ocopies[q] = c
    for d in range(1, nbo):
        peer = lax.rem(bo + d, nbo)
        c = remote(bpair, pall.at[bo], ps.at[d], pr.at[d],
                   {"beta": lax.div(peer, no), "orb": lax.rem(peer, no)})
        c.start()
        pcopies.append(c)

    vb[...] = jnp.zeros_like(vb)
    va[...] = jnp.zeros_like(va)
    gloc[...] = jnp.zeros_like(gloc)
    yabuf[...] = jnp.zeros_like(yabuf)

    def forward(q):
        for d in range(1, nb):
            xcopies[q, d].wait_recv()
            sect = section(q, lax.rem(b - d + nb, nb) * no + o)
            c = remote(sect, sect, fs.at[q, d], fr.at[q, d], {"orb": other})
            c.start()
            fcopies[q, d] = c

    def arrive(q):
        ocopies[q].wait_recv()
        for d in range(1, nb):
            fcopies[q, d].wait_recv()

    ry = capb * ROWT
    keep_b = lax.rem(iota((ry, ry), 0), ROWT) == lax.rem(iota((ry, ry), 1), ROWT)

    def beta_chunk(q):
        n = chunks[q]

        @pl.loop(0, tb)
        def _(u):
            for k in range(capb):
                s = u * capb + k
                img = dot_nt(panels[q][bsrc[s]], bcoup[s]).astype(BF16)
                for j in range(n // ROWT):
                    ybuf[k * ROWT:(k + 1) * ROWT, j * LANES:(j + 1) * LANES] = img[j * ROWT:(j + 1) * ROWT]
            y = ybuf[:, : n // ROWT * LANES]
            z = jnp.where(keep_b, dot_nt(y, y), 0.0)
            vb[u] += z.reshape(capb, ROWT, ry).sum(axis=1)

    slots_a = 8
    ra = slots_a * ROWT
    keep_a = lax.rem(iota((ra, ra), 0), ROWT) == lax.rem(iota((ra, ra), 1), ROWT)

    def alpha_all():
        @pl.loop(0, ta)
        def _(t):
            for k in range(capa):
                s = t * capa + k
                img = dot_nn(acoup[s], acol[asrc[s]]).astype(BF16)
                for j in range(LANES // ROWT):
                    yabuf[k * ROWT:(k + 1) * ROWT, j * width:(j + 1) * width] = img[j * ROWT:(j + 1) * ROWT]
            y = yabuf[...]
            z = jnp.where(keep_a, dot_nt(y, y), 0.0)
            va[t] = z.reshape(slots_a, ROWT, ra).sum(axis=1)

    forward(0)
    bcopy.wait()
    for q in range(nq):
        arrive(q)
        if q == nq - 1:
            break
        beta_chunk(q)
        forward(q + 1)
        if q == nq - 2:
            acopy.wait()
            owncols.wait()
            for c in acopies:
                c.wait_recv()
            alpha_all()
    beta_chunk(nq - 1)

    pb = LANES // capb
    gb = []
    for g in range(tb // pb):
        total = jnp.zeros((capb, LANES), F32)
        for i in range(pb):
            pick = (iota((ry, LANES), 1) == i * capb + lax.div(iota((ry, LANES), 0), ROWT)).astype(BF16)
            hi, lo = halves(vb[g * pb + i])
            total += dot_nn(hi, pick) + dot_nn(lo, pick)
        cnt = bcnt[g:g + 1, :]
        lane = lax.rem(iota((capb, LANES), 1), capb)
        gb.append(jnp.where((iota((capb, LANES), 0) < cnt) & (lane < cnt), total, 0.0))
    pa = LANES // slots_a
    ga = []
    for g in range(ta // pa):
        total = jnp.zeros((slots_a, LANES), F32)
        for i in range(pa):
            pick = (iota((ra, LANES), 1) == i * slots_a + lax.div(iota((ra, LANES), 0), ROWT)).astype(BF16)
            hi, lo = halves(va[g * pa + i])
            total += dot_nn(hi, pick) + dot_nn(lo, pick)
        cnt = acnt[g:g + 1, :]
        lane = lax.rem(iota((slots_a, LANES), 1), slots_a)
        ga.append(jnp.where((iota((slots_a, LANES), 0) < cnt) & (lane < cnt), total, 0.0))

    rb = capb * len(gb) // na
    rah = slots_a * len(ga) // na
    for j in range(na):
        lo = j * rb
        gloc[j, 0:rb, :] = gb[lo // capb][lo % capb:lo % capb + rb, :]
        lo = j * rah
        gloc[j, 4:4 + rah, :] = ga[lo // slots_a][lo % slots_a:lo % slots_a + rah, :]
    rcopies = []
    for d in range(1, na):
        peer = lax.rem(a + d, na)
        c = remote(gloc.at[peer], rsbuf.at[d], rss.at[d], rsr.at[d], {"alpha": peer})
        c.start()
        rcopies.append(c)
    piece = gloc[a]
    for d in range(1, na):
        rcopies[d - 1].wait_recv()
        piece += rsbuf[d]
    exbuf[a, bo] = piece
    ecopies = []
    for d in range(1, nbo):
        peer = lax.rem(bo + d, nbo)
        c = remote(exbuf.at[a, bo], exbuf.at[a, bo], exs.at[d], exr.at[d],
                   {"beta": lax.div(peer, no), "orb": lax.rem(peer, no)})
        c.start()
        ecopies.append(c)
    for c in ecopies:
        c.wait_recv()
    gcopies = []
    for d in range(1, na):
        c = remote(exbuf.at[a], exbuf.at[a], ags.at[d], agr.at[d], {"alpha": lax.rem(a + d, na)})
        c.start()
        gcopies.append(c)
    ownpair.wait()
    for c in pcopies:
        c.wait_recv()
    for c in gcopies:
        c.wait_recv()

    prows, qcols = out.shape[1], out.shape[2]
    pp, qq = up(prows, 16), up(qcols, LANES)
    p0, q0 = a * prows, bo * qcols

    def density(pairs, grams, size):
        total = jnp.zeros((pp, qq), F32)
        same = lax.div(iota((LANES, LANES), 0), size) == lax.div(iota((LANES, LANES), 1), size)
        for pair, gram in zip(pairs, grams):
            left = (iota((pp, LANES), 0) + p0 == pair).astype(BF16)
            right = (iota((qq, LANES), 0) + q0 == pair).astype(BF16)
            blocks = jnp.where(same, jnp.concatenate([gram] * (LANES // size), axis=0), 0.0)
            hi, lo = halves(blocks)
            hi, lo = halves(dot_nn(right, hi) + dot_nn(right, lo))
            total += dot_nt(left, hi) + dot_nt(left, lo)
        return total[:prows, :qcols]

    for j in range(na):
        for m in range(nbo):
            gsum[m, j * rb:(j + 1) * rb, :] = exbuf[j, m, 0:rb, :]
        ones = exbuf[j, 0, 4:4 + rah, :]
        for m in range(1, nbo):
            ones += exbuf[j, m, 4:4 + rah, :]
        gsum[nbo, j * rah:(j + 1) * rah, :] = ones
    out[0] = density(
        [apair[g:g + 1, :] for g in range(len(ga))],
        [gsum[nbo, g * slots_a:(g + 1) * slots_a, :] for g in range(len(ga))], slots_a)
    out[1] = density(
        [pall[m, g:g + 1, :] for m in range(nbo) for g in range(len(gb))],
        [gsum[m, g * capb:(g + 1) * capb, :] for m in range(nbo) for g in range(len(gb))], capb)

    for group in (list(xcopies.values()), list(ocopies.values()), list(fcopies.values()),
                  acopies, pcopies, rcopies, ecopies, gcopies):
        for c in group:
            c.wait_send()


def body(mesh, civec, acoup, asrc, apair, acnt, bcoup, bsrc, bpair, bcnt):
    na, nb, no = mesh.shape["alpha"], mesh.shape["beta"], mesh.shape["orb"]
    nbo = nb * no
    rows, cols = civec.shape
    ta, tb = acnt.shape[0], bcnt.shape[0]
    capa, capb = asrc.shape[0] // ta, bsrc.shape[0] // tb
    width = cols // na
    chunks = (rows // 2, rows // 2)
    nq = len(chunks)
    slots_a = 8
    apad = jnp.pad(apair.reshape(ta, capa), ((0, 0), (0, slots_a - capa)), constant_values=-1)
    apad = apad.reshape(-1, LANES)
    acnts = jnp.repeat(acnt, slots_a).reshape(-1, LANES)
    bcnts = jnp.repeat(bcnt, capb).reshape(-1, LANES)
    bpairs = bpair.reshape(-1, LANES)
    groups = bpairs.shape[0]
    cfg = (na, nb, no, chunks, capa, capb, ta, tb, width, cols)
    anyspace = pl.BlockSpec(memory_space=pl.ANY)
    vmem = pl.BlockSpec(memory_space=pltpu.VMEM)
    smem = pl.BlockSpec(memory_space=pltpu.SMEM)
    dma = pltpu.SemaphoreType.DMA
    return pl.pallas_call(
        functools.partial(kernel, cfg),
        out_shape=jax.ShapeDtypeStruct((2, NPAIR // na, NPAIR // nbo), F32),
        in_specs=[anyspace, anyspace, smem, vmem, vmem, anyspace, smem, vmem, vmem],
        out_specs=vmem,
        scratch_shapes=[pltpu.VMEM((cols * nbo // LANES, n, LANES), BF16) for n in chunks] + [
            pltpu.VMEM((rows * na // LANES, LANES, width), BF16),
            pltpu.VMEM(acoup.shape, BF16),
            pltpu.VMEM(bcoup.shape, BF16),
            pltpu.VMEM((capb * ROWT, max(chunks) // ROWT * LANES), BF16),
            pltpu.VMEM((slots_a * ROWT, LANES // ROWT * width), BF16),
            pltpu.VMEM((tb, capb, capb * ROWT), F32),
            pltpu.VMEM((ta, slots_a, slots_a * ROWT), F32),
            pltpu.VMEM((nbo, groups, LANES), jnp.int32),
            pltpu.VMEM((na, 8, LANES), F32),
            pltpu.VMEM((na, 8, LANES), F32),
            pltpu.VMEM((na, nbo, 8, LANES), F32),
            pltpu.VMEM((nbo + 1, groups * capb, LANES), F32),
            dma((4,)), dma((nq, cols // LANES)),
            dma((nq, nb)), dma((nq, nb)), dma((nq,)), dma((nq,)), dma((nq, nb)), dma((nq, nb)),
            dma((na,)), dma((na,)), dma((nbo,)), dma((nbo,)),
            dma((na,)), dma((na,)), dma((nbo,)), dma((nbo,)), dma((na,)), dma((na,)),
        ],
        compiler_params=pltpu.CompilerParams(
            collective_id=0, has_side_effects=True, vmem_limit_bytes=48 * 1024 * 1024),
    )(civec.reshape(-1, LANES, cols), acoup, asrc, apad, acnts, bcoup, bsrc, bpairs, bcnts)


def solution(mesh):
    return jax.shard_map(
        functools.partial(body, mesh),
        mesh=mesh,
        in_specs=(
            P(("frag", "alpha"), ("beta", "orb")),
            P("frag", None, None),
            P("frag"),
            P("frag"),
            P("frag"),
            P(("frag", "beta", "orb"), None, None),
            P(("frag", "beta", "orb")),
            P(("frag", "beta", "orb")),
            P(("frag", "beta", "orb")),
        ),
        out_specs=P("frag", "alpha", ("beta", "orb")),
        check_vma=False,
    )
```

time: 464 us -> 79.1 us (0.17)
  waiting for transfers between devices: 301 us -> 0 us
  local copies, waits for them, and re-layouts: 83.3 us -> 8.44 us
  Pallas kernels: 0 us -> 70.4 us
  matrix products: 58.6 us -> 0 us
  between operations: 14.5 us -> 0.04 us
  other arithmetic: 5.27 us -> 0 us
    unnamed x6 -> x0, waiting for transfers between devices: 225 us -> none
    all_gather x2 -> x0, waiting for transfers between devices: 76 us -> none  [the longest x1 45.1 us: body(): gathered = lax.all_gather(civec, 'alpha', axis=0, tiled=True)]
    pallas_call x0 -> x1, Pallas kernels: none -> 70.4 us  [body(): pl.pallas_call(functools.partial(kernel, cfg), out_shape=jax.ShapeDtypeSt...]
    dot_general x8 -> x0, matrix products: 58.6 us -> none  [the longest x1 17.5 us: body(): jnp.einsum('ukm,ulm->ukl', grouped, grouped, preferred_element_type=jnp.f...]
    reshape x3 -> x2, local copies, waits for them, and re-layouts: 45.5 us -> 0.83 us  [the longest x1 0.74 us: body(): apair.reshape(ta, capa)]
    gather x2 -> x0, local copies, waits for them, and re-layouts: 19.5 us -> none  [the longest x1 12 us: body(): picked = jnp.take(panel, beta_source, axis=1)]
    another operation x1, local copies, waits for them, and re-layouts: 5.4 us -> 0.09 us  [body(): acnts = jnp.repeat(acnt, slots_a).reshape(-1, LANES)]
  transfers between devices with their start and end apart: 4 -> 0, of which waited for: 4 -> 0; matrix products, arithmetic and copies ran while one was open for 19% -> 0% of each run, Pallas kernels for 0% -> 0%
where the time goes in v1:
time: 79.1 us; the launch traced here: 78.8 us
  Pallas kernels  70.4 us (89%)
  local copies, waits for them, and re-layouts  8.44 us (11%)
    pallas_call x1, Pallas kernels, body(): pl.pallas_call(functools.partial(kernel, cfg), out_shape=jax.ShapeDtypeSt...  70.4 us
    unnamed x10, local copies, waits for them, and re-layouts  5.12 us

profile of v1, /device:TPU:0, one launch (start us, length us, event | category | flops | bytes accessed | tf_op | source)
XLA Modules:
  0.0 78.8 jit_solution(4863925713710514510)
XLA Ops:
  0.0 0.7 broadcast_in_dim.11
  0.7 0.1 broadcast_in_dim.12
  0.8 0.1 broadcast_in_dim.13.bcnt
  0.9 0.7 reshape.15
  1.6 0.1 reshape.16.apair
  1.7 0.7 broadcast_in_dim.10
  2.5 0.1 reshape_reshape.4.acnt
  2.6 0.0 copy-start
  2.6 1.9 %copy-done = bf16[96,128,128]{2,1,0:T(8,128)(2,1)S(1)} copy-done((bf16[96,128,128]{2,1,0:T(8,128)(2,1)S(1)}, bf16[96,128,128]{2,1,0:T(8,128)(2,1)}, u32[]{:S(2)}) %copy-start) | copy-done | bytes 3145752
  4.5 0.0 copy-start.1
  4.5 1.2 %copy-done.1 = bf16[256,2048]{1,0:T(8,128)(2,1)S(1)} copy-done((bf16[256,2048]{1,0:T(8,128)(2,1)S(1)}, bf16[256,2048]{1,0:T(8,128)(2,1)}, u32[]{:S(2)}) %copy-start.1) | copy-done | bytes 1048600
  5.7 0.0 copy-start.2
  5.7 0.7 copy-done.2
  6.4 0.0 copy-start.3
  6.4 0.7 copy-done.3
  7.0 0.0 copy-start.4
  7.0 0.7 copy-done.4
  7.7 70.4 %shard_map.91 = f32[2,98,196]{2,1,0:T(8,128)S(1)} custom-call(bf16[2,128,2048]{2,1,0:T(8,128)(2,1)S(1)} %bitcast.2, bf16[96,128,128]{2,1,0:T(8,128)(2,1)S(1)} %copy-done, s32[96]{0:T(128)S(1)} %copy-done.4, s32[1,128]{1,0:T(1,128)S(1)} %reshape.16.apair, s32[1,128]{1,0:T(1,128)S(1)} %reshape_reshape.4.acnt, bf16[256,128,128]{2,1,0:T(8,128)(2,1)} %bcoup_hbm.1, ...), custom_call_target="tpu_custom_call" | custom-call | tf_op jit(solution)/shard_map/pallas_call | solution.py:315
  78.1 0.8 copy.11
  (1 shorter events, 0.0 us)
Async XLA Ops:
  2.6 1.9 %copy-start = (bf16[96,128,128]{2,1,0:T(8,128)(2,1)S(1)}, bf16[96,128,128]{2,1,0:T(8,128)(2,1)}, u32[]{:S(2)}) copy-start(bf16[96,128,128]{2,1,0:T(8,128)(2,1)} %acoup_hbm.1) | copy-start | bytes 9437188
  4.5 1.2 %copy-start.1 = (bf16[256,2048]{1,0:T(8,128)(2,1)S(1)}, bf16[256,2048]{1,0:T(8,128)(2,1)}, u32[]{:S(2)}) copy-start(bf16[256,2048]{1,0:T(8,128)(2,1)} %param.9) | copy-start | bytes 3145732
  5.7 0.7 copy-start.2
  6.4 0.7 copy-start.3
  7.0 0.7 copy-start.4

commit v2 on v1

v2 whole, which is shorter than its diff:
```python
import functools

import jax
import jax.numpy as jnp
from jax import lax
from jax.experimental import pallas as pl
from jax.experimental.pallas import tpu as pltpu
from jax.sharding import PartitionSpec as P

NPAIR = 784
MESH = pl.DeviceIdType.MESH
F32 = jnp.float32
BF16 = jnp.bfloat16
LANES = 128
ROWT = 16


def up(n, m):
    return -(-n // m) * m


def dot_nt(x, y):
    return lax.dot_general(x, y, (((1,), (1,)), ((), ())), preferred_element_type=F32)


def dot_nn(x, y):
    return jnp.dot(x, y, preferred_element_type=F32)


def halves(x):
    hi = x.astype(BF16)
    return hi, (x - hi.astype(F32)).astype(BF16)


def iota(shape, dim):
    return lax.broadcasted_iota(jnp.int32, shape, dim)


def kernel(
    cfg, civec, acoup_hbm, asrc_h, apair_h, acnt_h, bcoup_hbm, bsrc_h, bpair_h, bcnt_h, out, *scratch
):
    na, nb, no, chunks, ahead, capa, capb, ta, tb, width, cols = cfg
    nbo = nb * no
    nq = len(chunks)
    nc = width // LANES
    panels, acols = scratch[:nq], scratch[nq:nq + nc]
    (
        asrc, apairs, acnts, bsrc, bpairs, bcnts,
        acoup, bcoup, ybuf0, ybuf1, yabuf0, yabuf1, vb, va, pall, pbuf, qbuf, gloc, rsbuf, exbuf, gsum,
        lsem, csem, psem, xs, xr, os_, or_, fs, fr, als, alr, ps, pr, rss, rsr, exs, exr, ags, agr,
    ) = scratch[nq + nc:]
    a = lax.axis_index("alpha")
    b = lax.axis_index("beta")
    o = lax.axis_index("orb")
    bo = b * no + o
    other = 1 - o
    row0 = [sum(chunks[:q]) for q in range(nq)]

    wide = cols // LANES

    def section(q, which):
        return panels[q].at[pl.ds(which * wide, wide)]

    def remote(src, dst, ss, rs, dev):
        return pltpu.make_async_remote_copy(
            src_ref=src, dst_ref=dst, send_sem=ss, recv_sem=rs,
            device_id=dev, device_id_type=MESH,
        )

    local = [
        [
            pltpu.make_async_copy(
                civec.at[row0[q] // LANES, pl.ds(row0[q] % LANES, chunks[q]), pl.ds(i * LANES, LANES)],
                panels[q].at[bo * wide + i], psem.at[q, i])
            for i in range(wide)
        ]
        for q in range(nq)
    ]
    bcopy = pltpu.make_async_copy(bcoup_hbm, bcoup, lsem.at[0])
    acopy = pltpu.make_async_copy(acoup_hbm, acoup, lsem.at[1])
    tall = civec.shape[0]
    ownrows = pl.ds(a * tall, tall)

    def piece_of(which, c):
        return civec.at[:, :, pl.ds(pl.multiple_of(which * width + c * LANES, LANES), LANES)]

    owncols = [
        pltpu.make_async_copy(piece_of(a, c), acols[c].at[ownrows], csem.at[c]) for c in range(nc)
    ]
    lists = [
        pltpu.make_async_copy(src, dst, lsem.at[2 + i])
        for i, (src, dst) in enumerate((
            (asrc_h, asrc), (apair_h, apairs), (acnt_h, acnts),
            (bsrc_h, bsrc), (bpair_h, bpairs), (bcnt_h, bcnts)))
    ]

    barrier = pltpu.get_barrier_semaphore()
    for d in range(1, na):
        pl.semaphore_signal(barrier, inc=1, device_id={"alpha": lax.rem(a + d, na)}, device_id_type=MESH)
    for d in range(1, nbo):
        peer = lax.rem(bo + d, nbo)
        pl.semaphore_signal(
            barrier, inc=1,
            device_id={"beta": lax.div(peer, no), "orb": lax.rem(peer, no)}, device_id_type=MESH)
    for q in range(nq):
        for c in local[q]:
            c.start()
    for c in lists + owncols:
        c.start()
    bcopy.start()
    acopy.start()
    pl.semaphore_wait(barrier, na - 1 + nbo - 1)

    xcopies, ocopies, fcopies, acopies, pcopies = {}, {}, {}, {}, []

    def send_chunk(q):
        for c in local[q]:
            c.wait()
        mine = section(q, bo)
        for d in range(1, nb):
            c = remote(mine, mine, xs.at[q, d], xr.at[q, d], {"beta": lax.rem(b + d, nb)})
            c.start()
            xcopies[q, d] = c
        c = remote(mine, mine, os_.at[q], or_.at[q], {"orb": other})
        c.start()
        ocopies[q] = c

    def send_cols(c):
        for d in range(na - 1, 0, -1):
            peer = lax.rem(a + d, na)
            copy = remote(piece_of(peer, c), acols[c].at[ownrows], als.at[c, d], alr.at[c, d], {"alpha": peer})
            copy.start()
            acopies[c, d] = copy

    send_chunk(0)
    for c in range(nc):
        send_cols(c)

    def lane_row(values):
        lanes = iota((1, LANES), 1)
        row = jnp.full((1, LANES), -1, jnp.int32)
        for lane, value in values:
            row = jnp.where(lanes == lane, value, row)
        return row

    def span_row(values, size):
        lanes = lax.div(iota((1, LANES), 1), size)
        row = jnp.zeros((1, LANES), jnp.int32)
        for i, value in enumerate(values):
            row = jnp.where(lanes == i, value, row)
        return row

    slots_a = 8
    pa, pb = LANES // slots_a, LANES // capb
    na_g, nb_g = ta // pa, tb // pb
    for c in lists:
        c.wait()
    for g in range(nb_g):
        pall[bo, g:g + 1, :] = lane_row([(i, bpairs[g * LANES + i]) for i in range(LANES)])
    apair = [
        lane_row([(i * slots_a + k, apairs[(g * pa + i) * capa + k]) for i in range(pa) for k in range(capa)])
        for g in range(na_g)
    ]
    acnt = [span_row([acnts[g * pa + i] for i in range(pa)], slots_a) for g in range(na_g)]
    bcnt = [span_row([bcnts[g * pb + i] for i in range(pb)], capb) for g in range(nb_g)]
    for d in range(1, nbo):
        peer = lax.rem(bo + d, nbo)
        c = remote(pall.at[bo], pall.at[bo], ps.at[d], pr.at[d],
                   {"beta": lax.div(peer, no), "orb": lax.rem(peer, no)})
        c.start()
        pcopies.append(c)

    for q in range(1, min(ahead, nq)):
        send_chunk(q)

    vb[...] = jnp.zeros_like(vb)
    va[...] = jnp.zeros_like(va)
    gloc[...] = jnp.zeros_like(gloc)
    yabuf0[...] = jnp.zeros_like(yabuf0)
    yabuf1[...] = jnp.zeros_like(yabuf1)

    def forward(q):
        for d in range(1, nb):
            xcopies[q, d].wait_recv()
            sect = section(q, lax.rem(b - d + nb, nb) * no + o)
            c = remote(sect, sect, fs.at[q, d], fr.at[q, d], {"orb": other})
            c.start()
            fcopies[q, d] = c

    def arrive(q):
        ocopies[q].wait_recv()
        for d in range(1, nb):
            fcopies[q, d].wait_recv()

    ry = capb * ROWT
    keep_b = lax.rem(iota((ry, ry), 0), ROWT) == lax.rem(iota((ry, ry), 1), ROWT)

    def beta_chunk(q):
        n = chunks[q]

        def images(u, ybuf):
            for k in range(capb):
                s = u * capb + k
                img = dot_nn(panels[q][bsrc[s]], bcoup[s]).astype(BF16)
                for j in range(n // ROWT):
                    ybuf[k * ROWT:(k + 1) * ROWT, j * LANES:(j + 1) * LANES] = img[j * ROWT:(j + 1) * ROWT]

        def gram(u, ybuf):
            y = ybuf[:, : n // ROWT * LANES]
            z = jnp.where(keep_b, dot_nt(y, y), 0.0)
            vb[u] += z.reshape(capb, ROWT, ry).sum(axis=1)

        images(0, ybuf0)

        @pl.loop(0, tb // 2)
        def _(i):
            images(2 * i + 1, ybuf1)
            gram(2 * i, ybuf0)
            images(lax.rem(2 * i + 2, tb), ybuf0)
            gram(2 * i + 1, ybuf1)

    ra = slots_a * ROWT
    keep_a = lax.rem(iota((ra, ra), 0), ROWT) == lax.rem(iota((ra, ra), 1), ROWT)

    def alpha_chunk(c):
        acopies_c = [acopies[c, d] for d in range(1, na)]
        owncols[c].wait()
        for copy in acopies_c:
            copy.wait_recv()

        def images(t, ybuf):
            for k in range(capa):
                s = t * capa + k
                img = dot_nn(acoup[s], acols[c][asrc[s]]).astype(BF16)
                for j in range(LANES // ROWT):
                    ybuf[k * ROWT:(k + 1) * ROWT, j * LANES:(j + 1) * LANES] = img[j * ROWT:(j + 1) * ROWT]

        def gram(t, ybuf):
            y = ybuf[...]
            z = jnp.where(keep_a, dot_nt(y, y), 0.0)
            va[t] += z.reshape(slots_a, ROWT, ra).sum(axis=1)

        images(0, yabuf0)

        @pl.loop(0, ta // 2)
        def _(i):
            images(2 * i + 1, yabuf1)
            gram(2 * i, yabuf0)
            images(lax.rem(2 * i + 2, ta), yabuf0)
            gram(2 * i + 1, yabuf1)

    bcopy.wait()

    @pl.loop(0, bcoup.shape[0] // 8)
    def _(i):
        for k in range(8):
            bcoup[i * 8 + k] = bcoup[i * 8 + k].T

    prows, qcols = out.shape[1], out.shape[2]
    pp, qq = up(prows, 16), up(qcols, LANES)
    p0, q0 = a * prows, bo * qcols
    ngb = nbo * nb_g
    def onehots():
        for c in pcopies:
            c.wait_recv()
        for g in range(ngb + na_g):
            pair = pall[g // nb_g, g % nb_g:g % nb_g + 1, :] if g < ngb else apair[g - ngb]
            pbuf[:, g * LANES:(g + 1) * LANES] = (iota((pp, LANES), 0) + p0 == pair).astype(BF16)
            qbuf[g] = (iota((qq, LANES), 0) + q0 == pair).astype(F32).T.astype(BF16)

    done_a = 0
    for q in range(nq):
        if q == nq - 1:
            onehots()
            acopy.wait()
            while done_a < nc - 1:
                alpha_chunk(done_a)
                done_a += 1
        forward(q)
        if q + ahead < nq:
            send_chunk(q + ahead)
        if q == nq - 1:
            while done_a < nc:
                alpha_chunk(done_a)
                done_a += 1
        arrive(q)
        beta_chunk(q)

    def side_by_side(v, size, counts):
        n = LANES // size
        pick = lax.rem(iota((size * ROWT, LANES), 1), size) == lax.div(iota((size * ROWT, LANES), 0), ROWT)
        hi, lo = halves(v[...].reshape(-1, size * ROWT))
        total = dot_nn(jnp.concatenate([hi, lo], axis=1), jnp.concatenate([pick.astype(BF16)] * 2, axis=0))
        lanes, slot = iota((size, LANES), 1), iota((size, LANES), 0)
        grams = []
        for g, cnt in enumerate(counts):
            gram = jnp.zeros((size, LANES), F32)
            for i in range(n):
                r = (g * n + i) * size
                gram = jnp.where(lax.div(lanes, size) == i, total[r:r + size], gram)
            grams.append(jnp.where((slot < cnt) & (lax.rem(lanes, size) < cnt), gram, 0.0))
        return grams

    gb = side_by_side(vb, capb, bcnt)
    ga = side_by_side(va, slots_a, acnt)

    rb = capb * len(gb) // na
    rah = slots_a * len(ga) // na
    for j in range(na):
        lo = j * rb
        gloc[j, 0:rb, :] = gb[lo // capb][lo % capb:lo % capb + rb, :]
        lo = j * rah
        gloc[j, 4:4 + rah, :] = ga[lo // slots_a][lo % slots_a:lo % slots_a + rah, :]
    rcopies = []
    for d in range(1, na):
        peer = lax.rem(a + d, na)
        c = remote(gloc.at[peer], rsbuf.at[d], rss.at[d], rsr.at[d], {"alpha": peer})
        c.start()
        rcopies.append(c)
    piece = gloc[a]
    for d in range(1, na):
        rcopies[d - 1].wait_recv()
        piece += rsbuf[d]
    exbuf[a, bo] = piece
    ecopies = []
    for d in range(1, nbo):
        peer = lax.rem(bo + d, nbo)
        c = remote(exbuf.at[a, bo], exbuf.at[a, bo], exs.at[d], exr.at[d],
                   {"beta": lax.div(peer, no), "orb": lax.rem(peer, no)})
        c.start()
        ecopies.append(c)
    for c in ecopies:
        c.wait_recv()
    gcopies = []
    for d in range(1, na):
        c = remote(exbuf.at[a], exbuf.at[a], ags.at[d], agr.at[d], {"alpha": lax.rem(a + d, na)})
        c.start()
        gcopies.append(c)
    for c in gcopies:
        c.wait_recv()

    def density(grams, first, size):
        same = lax.div(iota((LANES, LANES), 0), size) == lax.div(iota((LANES, LANES), 1), size)
        his, los = [], []
        for i, gram in enumerate(grams):
            blocks = jnp.where(same, jnp.concatenate([gram] * (LANES // size), axis=0), 0.0)
            hi, lo = halves(blocks)
            right = qbuf[first + i]
            hi, lo = halves(dot_nn(
                jnp.concatenate([hi, lo], axis=1), jnp.concatenate([right, right], axis=0)))
            his.append(hi)
            los.append(lo)
        left = pbuf[:, first * LANES:(first + len(grams)) * LANES]
        total = dot_nn(left, jnp.concatenate(his, axis=0)) + dot_nn(left, jnp.concatenate(los, axis=0))
        return total[:prows, :qcols]

    for j in range(na):
        for m in range(nbo):
            gsum[m, j * rb:(j + 1) * rb, :] = exbuf[j, m, 0:rb, :]
        ones = exbuf[j, 0, 4:4 + rah, :]
        for m in range(1, nbo):
            ones += exbuf[j, m, 4:4 + rah, :]
        gsum[nbo, j * rah:(j + 1) * rah, :] = ones
    out[0] = density([gsum[nbo, g * slots_a:(g + 1) * slots_a, :] for g in range(na_g)], ngb, slots_a)
    out[1] = density(
        [gsum[m, g * capb:(g + 1) * capb, :] for m in range(nbo) for g in range(nb_g)], 0, capb)

    for group in (list(xcopies.values()), list(ocopies.values()), list(fcopies.values()),
                  list(acopies.values()), pcopies, rcopies, ecopies, gcopies):
        for c in group:
            c.wait_send()


def body(mesh, civec, acoup, asrc, apair, acnt, bcoup, bsrc, bpair, bcnt):
    na, nb, no = mesh.shape["alpha"], mesh.shape["beta"], mesh.shape["orb"]
    nbo = nb * no
    rows, cols = civec.shape
    ta, tb = acnt.shape[0], bcnt.shape[0]
    capa, capb = asrc.shape[0] // ta, bsrc.shape[0] // tb
    width = cols // na
    chunks = (rows // 2, rows // 2)
    ahead = len(chunks)
    nq, nc = len(chunks), width // LANES
    slots_a = 8
    groups, groups_a = bpair.shape[0] // LANES, ta * slots_a // LANES
    cfg = (na, nb, no, chunks, ahead, capa, capb, ta, tb, width, cols)
    anyspace = pl.BlockSpec(memory_space=pl.ANY)
    vmem = pl.BlockSpec(memory_space=pltpu.VMEM)
    dma = pltpu.SemaphoreType.DMA
    return pl.pallas_call(
        functools.partial(kernel, cfg),
        out_shape=jax.ShapeDtypeStruct((2, NPAIR // na, NPAIR // nbo), F32),
        in_specs=[anyspace] * 9,
        out_specs=vmem,
        scratch_shapes=[pltpu.VMEM((cols * nbo // LANES, n, LANES), BF16) for n in chunks] + [
            pltpu.VMEM((rows * na // LANES, LANES, LANES), BF16) for _ in range(nc)] + [
            pltpu.SMEM(x.shape, jnp.int32) for x in (asrc, apair, acnt, bsrc, bpair, bcnt)] + [
            pltpu.VMEM(acoup.shape, BF16),
            pltpu.VMEM(bcoup.shape, BF16),
            pltpu.VMEM((capb * ROWT, max(chunks) // ROWT * LANES), BF16),
            pltpu.VMEM((capb * ROWT, max(chunks) // ROWT * LANES), BF16),
            pltpu.VMEM((slots_a * ROWT, LANES // ROWT * LANES), BF16),
            pltpu.VMEM((slots_a * ROWT, LANES // ROWT * LANES), BF16),
            pltpu.VMEM((tb, capb, capb * ROWT), F32),
            pltpu.VMEM((ta, slots_a, slots_a * ROWT), F32),
            pltpu.VMEM((nbo, groups, LANES), jnp.int32),
            pltpu.VMEM((up(NPAIR // na, 16), (nbo * groups + groups_a) * LANES), BF16),
            pltpu.VMEM((nbo * groups + groups_a, LANES, up(NPAIR // nbo, LANES)), BF16),
            pltpu.VMEM((na, 8, LANES), F32),
            pltpu.VMEM((na, 8, LANES), F32),
            pltpu.VMEM((na, nbo, 8, LANES), F32),
            pltpu.VMEM((nbo + 1, groups * capb, LANES), F32),
            dma((8,)), dma((nc,)), dma((nq, cols // LANES)),
            dma((nq, nb)), dma((nq, nb)), dma((nq,)), dma((nq,)), dma((nq, nb)), dma((nq, nb)),
            dma((nc, na)), dma((nc, na)), dma((nbo,)), dma((nbo,)),
            dma((na,)), dma((na,)), dma((nbo,)), dma((nbo,)), dma((na,)), dma((na,)),
        ],
        compiler_params=pltpu.CompilerParams(
            collective_id=0, has_side_effects=True, vmem_limit_bytes=60 * 1024 * 1024),
    )(civec.reshape(-1, LANES, cols), acoup, asrc, apair, acnt, bcoup, bsrc, bpair, bcnt)


def solution(mesh):
    return jax.shard_map(
        functools.partial(body, mesh),
        mesh=mesh,
        in_specs=(
            P(("frag", "alpha"), ("beta", "orb")),
            P("frag", None, None),
            P("frag"),
            P("frag"),
            P("frag"),
            P(("frag", "beta", "orb"), None, None),
            P(("frag", "beta", "orb")),
            P(("frag", "beta", "orb")),
            P(("frag", "beta", "orb")),
        ),
        out_specs=P("frag", "alpha", ("beta", "orb")),
        check_vma=False,
    )
```

time: 79.1 us -> 57.8 us (0.73)
  Pallas kernels: 70.4 us -> 55.9 us
  local copies, waits for them, and re-layouts: 8.44 us -> 1.71 us
    pallas_call x1, Pallas kernels: 70.4 us -> 55.9 us  [body(): pl.pallas_call(functools.partial(kernel, cfg), out_shape=jax.ShapeDtypeSt...]
    unnamed x10 -> x0, local copies, waits for them, and re-layouts: 5.12 us -> none
    broadcast_in_dim x4 -> x0, local copies, waits for them, and re-layouts: 1.62 us -> none  [the longest x3 0.89 us: body(): bcnts = jnp.repeat(bcnt, capb).reshape(-1, LANES)]
    pallas_call x1, local copies, waits for them, and re-layouts: 0.78 us -> 1.71 us  [body(): pl.pallas_call(functools.partial(kernel, cfg), out_shape=jax.ShapeDtypeSt...]
    reshape x2 -> x0, local copies, waits for them, and re-layouts: 0.83 us -> none  [the longest x1 0.74 us: body(): apair.reshape(ta, capa)]
where the time goes in v2:
time: 57.8 us; the launch traced here: 57.6 us
  Pallas kernels  55.9 us (97%)
  local copies, waits for them, and re-layouts  1.71 us (3%)
    pallas_call x1, Pallas kernels, body(): pl.pallas_call(functools.partial(kernel, cfg), out_shape=jax.ShapeDtypeSt...  55.9 us
    pallas_call x1, local copies, waits for them, and re-layouts, body(): pl.pallas_call(functools.partial(kernel, cfg), out_shape=jax.ShapeDtypeSt...  1.71 us

profile of v2, /device:TPU:0, one launch (start us, length us, event | category | flops | bytes accessed | tf_op | source)
XLA Modules:
  0.0 57.6 jit_solution(2811417216559016107)
XLA Ops:
  0.0 55.9 %shard_map.91 = f32[2,98,196]{2,1,0:T(8,128)} custom-call(bf16[2,128,2048]{2,1,0:T(8,128)(2,1)} %bitcast.1, bf16[96,128,128]{2,1,0:T(8,128)(2,1)} %acoup_hbm.1, s32[96]{0:T(128)} %asrc_h.1, s32[96]{0:T(128)} %apair_h.1, s32[16]{0:T(128)} %acnt_h.1, bf16[256,128,128]{2,1,0:T(8,128)(2,1)} %bcoup_hbm.1, s32[256]{0:T(256)} %bsrc_h.1, s32[256]{0:T(256)} %bpair_h.1, ...), custom_call_target="tpu_custom_call" | custom-call | tf_op jit(solution)/shard_map/pallas_call | solution.py:390
  55.9 1.7 %copy.10 = f32[2,98,196]{2,0,1:T(2,128)} copy(f32[2,98,196]{2,1,0:T(8,128)} %shard_map.91) | data formatting | bytes 307328 | tf_op jit(solution)/shard_map/pallas_call | solution.py:390

commit v3 on v2

--- a/solution.py
+++ b/solution.py
@@ -47,7 +47,7 @@
     (
         asrc, apairs, acnts, bsrc, bpairs, bcnts,
         acoup, bcoup, ybuf0, ybuf1, yabuf0, yabuf1, vb, va, pall, pbuf, qbuf, gloc, rsbuf, exbuf, gsum,
-        lsem, csem, psem, xs, xr, os_, or_, fs, fr, als, alr, ps, pr, rss, rsr, exs, exr, ags, agr,
+        lsem, csem, psem, xs, xr, os_, or_, fs, fr, als, alr, ps, pr, rss, rsr, exs, exr,
     ) = scratch[nq + nc:]
     a = lax.axis_index("alpha")
     b = lax.axis_index("beta")
@@ -95,13 +95,16 @@
     ]
 
     barrier = pltpu.get_barrier_semaphore()
-    for d in range(1, na):
-        pl.semaphore_signal(barrier, inc=1, device_id={"alpha": lax.rem(a + d, na)}, device_id_type=MESH)
-    for d in range(1, nbo):
-        peer = lax.rem(bo + d, nbo)
-        pl.semaphore_signal(
-            barrier, inc=1,
-            device_id={"beta": lax.div(peer, no), "orb": lax.rem(peer, no)}, device_id_type=MESH)
+    everyone = na * nbo
+
+    def device(d):
+        peer_a, peer = lax.rem(a + lax.div(d, nbo), na), lax.rem(bo + lax.rem(d, nbo), nbo)
+        return {"alpha": peer_a, "beta": lax.div(peer, no), "orb": lax.rem(peer, no)}
+
+    @pl.loop(1, everyone)
+    def _(d):
+        pl.semaphore_signal(barrier, inc=1, device_id=device(d), device_id_type=MESH)
+
     for q in range(nq):
         for c in local[q]:
             c.start()
@@ -109,7 +112,7 @@
         c.start()
     bcopy.start()
     acopy.start()
-    pl.semaphore_wait(barrier, na - 1 + nbo - 1)
+    pl.semaphore_wait(barrier, everyone - 1)
 
     xcopies, ocopies, fcopies, acopies, pcopies = {}, {}, {}, {}, []
 
@@ -322,22 +325,17 @@
         rcopies[d - 1].wait_recv()
         piece += rsbuf[d]
     exbuf[a, bo] = piece
-    ecopies = []
-    for d in range(1, nbo):
-        peer = lax.rem(bo + d, nbo)
-        c = remote(exbuf.at[a, bo], exbuf.at[a, bo], exs.at[d], exr.at[d],
-                   {"beta": lax.div(peer, no), "orb": lax.rem(peer, no)})
-        c.start()
-        ecopies.append(c)
-    for c in ecopies:
-        c.wait_recv()
-    gcopies = []
-    for d in range(1, na):
-        c = remote(exbuf.at[a], exbuf.at[a], ags.at[d], agr.at[d], {"alpha": lax.rem(a + d, na)})
-        c.start()
-        gcopies.append(c)
-    for c in gcopies:
-        c.wait_recv()
+
+    def spread(d):
+        return remote(exbuf.at[a, bo], exbuf.at[a, bo], exs.at[d], exr.at[d], device(d))
+
+    @pl.loop(1, everyone)
+    def _(d):
+        spread(d).start()
+
+    @pl.loop(1, everyone)
+    def _(d):
+        spread(d).wait_recv()
 
     def density(grams, first, size):
         same = lax.div(iota((LANES, LANES), 0), size) == lax.div(iota((LANES, LANES), 1), size)
@@ -366,9 +364,13 @@
         [gsum[m, g * capb:(g + 1) * capb, :] for m in range(nbo) for g in range(nb_g)], 0, capb)
 
     for group in (list(xcopies.values()), list(ocopies.values()), list(fcopies.values()),
-                  list(acopies.values()), pcopies, rcopies, ecopies, gcopies):
+                  list(acopies.values()), pcopies, rcopies):
         for c in group:
             c.wait_send()
+
+    @pl.loop(1, everyone)
+    def _(d):
+        spread(d).wait_send()
 
 
 def body(mesh, civec, acoup, asrc, apair, acnt, bcoup, bsrc, bpair, bcnt):
@@ -413,7 +415,7 @@
             dma((8,)), dma((nc,)), dma((nq, cols // LANES)),
             dma((nq, nb)), dma((nq, nb)), dma((nq,)), dma((nq,)), dma((nq, nb)), dma((nq, nb)),
             dma((nc, na)), dma((nc, na)), dma((nbo,)), dma((nbo,)),
-            dma((na,)), dma((na,)), dma((nbo,)), dma((nbo,)), dma((na,)), dma((na,)),
+            dma((na,)), dma((na,)), dma((na * nbo,)), dma((na * nbo,)),
         ],
         compiler_params=pltpu.CompilerParams(
             collective_id=0, has_side_effects=True, vmem_limit_bytes=60 * 1024 * 1024),

time: 57.8 us -> 57.3 us (level)
  no operation moved by 1% of the time
where the time goes in v3:
time: 57.3 us; the launch traced here: 57.2 us
  Pallas kernels  55.5 us (97%)
  local copies, waits for them, and re-layouts  1.71 us (3%)
    pallas_call x1, Pallas kernels, body(): pl.pallas_call(functools.partial(kernel, cfg), out_shape=jax.ShapeDtypeSt...  55.5 us
    pallas_call x1, local copies, waits for them, and re-layouts, body(): pl.pallas_call(functools.partial(kernel, cfg), out_shape=jax.ShapeDtypeSt...  1.71 us

profile of v3, /device:TPU:0, one launch (start us, length us, event | category | flops | bytes accessed | tf_op | source)
XLA Modules:
  0.0 57.2 jit_solution(9935786923120928106)
XLA Ops:
  0.0 55.5 %shard_map.91 = f32[2,98,196]{2,1,0:T(8,128)} custom-call(bf16[2,128,2048]{2,1,0:T(8,128)(2,1)} %bitcast.1, bf16[96,128,128]{2,1,0:T(8,128)(2,1)} %acoup_hbm.1, s32[96]{0:T(128)} %asrc_h.1, s32[96]{0:T(128)} %apair_h.1, s32[16]{0:T(128)} %acnt_h.1, bf16[256,128,128]{2,1,0:T(8,128)(2,1)} %bcoup_hbm.1, s32[256]{0:T(256)} %bsrc_h.1, s32[256]{0:T(256)} %bpair_h.1, ...), custom_call_target="tpu_custom_call" | custom-call | tf_op jit(solution)/shard_map/pallas_call | solution.py:392
  55.5 1.7 %copy.10 = f32[2,98,196]{2,0,1:T(2,128)} copy(f32[2,98,196]{2,1,0:T(8,128)} %shard_map.91) | data formatting | bytes 307328 | tf_op jit(solution)/shard_map/pallas_call | solution.py:392
